TPU v7x, 32 devices: a whole 2x2x4 slice. The times are simulated.
32 devices in a mesh: blk: 8 (over y, x, core), grp: 4 (over z).
Axes of the slice: x: 2, y: 2, z: 4, core: 2. Of those that a mesh axis runs over, the one named last changes fastest.
Arguments:
- queries: float32 [4096, 1024], P(('blk', 'grp')), may hold values from -48 to 48
- passages: float32 [4096, 1024], P(('blk', 'grp')), may hold values from -48 to 48
- hard_table: bfloat16 [24576, 1024], P(('blk', 'grp')), may hold values from -12 to 12
- hard_index: int32 [4096, 8], P(('blk', 'grp')), may hold values from 0 to 3071, as said below
Outputs:
- mean_loss: float32 [], replicated
- query_grad: float32 [4096, 1024], P(('blk', 'grp'))
- passage_grad: float32 [4096, 1024], P(('blk', 'grp'))
- table_grad: bfloat16 [24576, 1024], P(('blk', 'grp'))
Inputs may be any that keep to these rules, and one draw needn't show every extreme that they name: Owner o = hard_index // 768 is a batch group of the query's own loop shard. Among the 1024 entries of one device, the four owners are named exactly 384, 256, 256 and 128 times in some order, and the owner named 3 * 128 times is the same for all devices of one loop shard; entries may repeat.
All inputs are finite; a program needn't handle non-finite values.
Results may differ from a plain program's by a relative error of at most 0.0038.
Values may be sent and summed in bfloat16 or wider, within the bound.
A program may use at most 64 MiB of HBM per device.

v0:
```python
import jax
import jax.numpy as jnp
from jax import lax
from jax.sharding import PartitionSpec as P

STOPS = 4


score_scale = 0.015625


def passed_along(value, axis, by):
    length = lax.axis_size(axis)
    return lax.ppermute(value, axis, [(i, (i + by) % length) for i in range(length)])


def pair_scores(query_blk, passage_block):
    return (
        lax.dot_general(
            query_blk,
            passage_block,
            (((1,), (1,)), ((), ())),
            precision=lax.Precision.HIGHEST,
            preferred_element_type=jnp.float32,
        )
        * score_scale
    )


def weighted_rows(weight, passage_block):
    return jnp.dot(
        weight, passage_block, precision=lax.Precision.HIGHEST, preferred_element_type=jnp.float32
    )


def weighted_queries(weight, query_blk):
    return lax.dot_general(
        weight,
        query_blk,
        (((0,), (0,)), ((), ())),
        precision=lax.Precision.HIGHEST,
        preferred_element_type=jnp.float32,
    )


def local(queries, passages, hard_table, hard_index):
    row_count, feature_width = queries.shape
    group_count = lax.axis_size("grp")
    table_rows = hard_table.shape[0]
    slot_count = hard_index.shape[1]
    capacity = 3 * row_count
    flat_index = hard_index.reshape(-1)
    owner_id = flat_index // table_rows
    row_within = flat_index % table_rows
    owner_hot = (owner_id[:, None] == jnp.arange(group_count, dtype=jnp.int32)[None, :]).astype(
        jnp.int32
    )
    before = jnp.cumsum(owner_hot, axis=0) - owner_hot
    slot_rank = jnp.sum(before * owner_hot, axis=1)
    slot_dest = owner_id * capacity + slot_rank
    request = jnp.zeros((group_count * capacity,), jnp.int32).at[slot_dest].set(row_within)
    request = request.reshape(group_count, capacity)
    asked = lax.all_to_all(request, "grp", split_axis=0, concat_axis=0, tiled=True)
    picked = jnp.take(hard_table, asked, axis=0)
    returned = lax.all_to_all(picked, "grp", split_axis=0, concat_axis=0, tiled=True)
    hard_vecs = returned.reshape(group_count * capacity, feature_width)[slot_dest]
    hard_vecs = hard_vecs.reshape(row_count, slot_count, feature_width).astype(jnp.float32)
    hard_scores = (
        jnp.einsum("rd,rkd->rk", queries, hard_vecs, precision=lax.Precision.HIGHEST) * score_scale
    )
    positive = jnp.sum(queries * passages, axis=1) * score_scale
    run_max = jnp.max(hard_scores, axis=1)
    run_sum = jnp.sum(jnp.exp(hard_scores - run_max[:, None]), axis=1)
    passage_block = passages
    for stop_index in range(STOPS):
        if stop_index > 0:
            passage_block = passed_along(passage_block, "blk", 1)
        block_scores = pair_scores(queries, passage_block)
        new_max = jnp.maximum(run_max, jnp.max(block_scores, axis=1))
        run_sum = run_sum * jnp.exp(run_max - new_max) + jnp.sum(
            jnp.exp(block_scores - new_max[:, None]), axis=1
        )
        run_max = new_max
    lse = run_max + jnp.log(run_sum)
    device_count = lax.axis_size("blk") * lax.axis_size("grp")
    total_loss = lax.psum(jnp.sum(lse - positive), ("blk", "grp"))
    mean_loss = total_loss / (row_count * device_count)
    hard_weight = jnp.exp(hard_scores - lse[:, None])
    query_accum = jnp.einsum("rk,rkd->rd", hard_weight, hard_vecs, precision=lax.Precision.HIGHEST)
    passage_block = passages
    grad_accum = jnp.zeros((row_count, feature_width), jnp.float32)
    for stop_index in range(STOPS):
        if stop_index > 0:
            passage_block, grad_accum = passed_along((passage_block, grad_accum), "blk", 1)
        weight = jnp.exp(pair_scores(queries, passage_block) - lse[:, None])
        query_accum = query_accum + weighted_rows(weight, passage_block)
        grad_accum = grad_accum + weighted_queries(weight, queries)
    grad_accum = passed_along(grad_accum, "blk", -(STOPS - 1))
    query_grad = score_scale * (query_accum - passages)
    passage_grad = score_scale * grad_accum - score_scale * queries
    hard_term = (score_scale * hard_weight[:, :, None] * queries[:, None, :]).astype(jnp.bfloat16)
    outgoing = jnp.zeros((group_count * capacity, feature_width), jnp.bfloat16)
    outgoing = outgoing.at[slot_dest].set(hard_term.reshape(row_count * slot_count, feature_width))
    outgoing = outgoing.reshape(group_count, capacity, feature_width)
    incoming = lax.all_to_all(outgoing, "grp", split_axis=0, concat_axis=0, tiled=True)
    table_accum = jnp.zeros((table_rows, feature_width), jnp.float32)
    table_accum = table_accum.at[asked.reshape(-1)].add(
        incoming.reshape(group_count * capacity, feature_width).astype(jnp.float32)
    )
    return (mean_loss, query_grad, passage_grad, table_accum.astype(jnp.bfloat16))


def solution(mesh):
    return jax.shard_map(
        local,
        mesh=mesh,
        in_specs=(
            P(("blk", "grp"), None),
            P(("blk", "grp"), None),
            P(("blk", "grp"), None),
            P(("blk", "grp"), None),
        ),
        out_specs=(P(), P(("blk", "grp"), None), P(("blk", "grp"), None), P(("blk", "grp"), None)),
        check_vma=False,
    )
```

profile of v0, /device:TPU:0, one launch (start us, length us, event | category | flops | bytes accessed | tf_op | source)
XLA Modules:
  0.0 256.8 jit_solution(13997987347748642262)
XLA Ops:
  0.6 0.8 compare_and_fusion.1
  1.5 0.7 broadcast_remainder_fusion
  2.9 1.1 reduce-window.6
  5.0 4.3 %scatter_custom_fusion = s32[1536]{0:T(1024)S(1)} fusion(s32[1024]{0:T(1024)S(1)} %bitcast.76, s32[1024]{0:T(1024)S(1)} %get-tuple-element.14, s32[]{:T(128)} %constant.22.clone.1), kind=kCustom, calls=%fused_computation.80 | custom fusion | bytes 6148 | tf_op jit(solution)/shard_map/scatter | solution.py:61
  9.4 11.7 %all_to_all.25 = s32[4,1,384]{2,1,0:T(1,128)S(1)} all-to-all(s32[4,1,384]{2,1,0:T(1,128)S(1)} %all_to_all.16), channel_id=1, replica_groups=mesh['blk'=8,'grp'=4] {'grp'}, dimensions={0} | all-to-all | bytes 12288 | tf_op jit(solution)/shard_map/all_to_all | solution.py:63
  21.2 5.8 %gather_fusion = bf16[1536,1024]{1,0:T(8,128)(2,1)} fusion(bf16[768,1024]{1,0:T(8,128)(2,1)S(1)} %copy-done, s32[2048]{0:T(1024)S(1)} %pad_clamp_fusion), kind=kCustom, calls=%fused_computation | custom fusion | bytes 6297600 | tf_op jit(solution)/shard_map/jit(_take)/gather | solution.py:64
  27.0 3.4 %broadcast_select_fusion = bf16[4,384,1024]{2,1,0:T(8,128)(2,1)} fusion(bf16[4,384,1024]{2,1,0:T(8,128)(2,1)} %bitcast.70, pred[4,384]{1,0:T(4,128)(4,1)S(1)} %compare_and_fusion), kind=kLoop, calls=%fused_computation.9 | loop fusion | flops 1572864 | bytes 6292992 | tf_op jit(solution)/shard_map/jit(_take)/select_n | solution.py:64
  30.4 4.8 %all-to-all-start.1 = ((bf16[4,384,1024]{2,1,0:T(8,128)(2,1)}), bf16[4,384,1024]{2,1,0:T(8,128)(2,1)}, u32[]{:S(2)}, u32[]{:S(2)}) async-start(bf16[4,384,1024]{2,1,0:T(8,128)(2,1)} %broadcast_select_fusion), calls=%async_computation.1 | async-start | bytes 6291456 | tf_op jit(solution)/shard_map/all_to_all | solution.py:65
  35.2 9.5 %collective-permute-done = f32[128,1024]{1,0:T(8,128)S(1)} collective-permute-done((f32[128,1024]{1,0:T(8,128)S(1)}, f32[128,1024]{1,0:T(8,128)S(1)}, u32[]{:S(2)}, u32[]{:S(2)}) %collective-permute-start) | collective-permute-done | bytes 524320 | tf_op jit(solution)/shard_map/ppermute | solution.py:14
  45.3 8.9 %collective-permute-done.1 = f32[128,1024]{1,0:T(8,128)S(1)} collective-permute-done((f32[128,1024]{1,0:T(8,128)S(1)}, f32[128,1024]{1,0:T(8,128)S(1)}, u32[]{:S(2)}, u32[]{:S(2)}) %collective-permute-start.1) | collective-permute-done | bytes 524320 | tf_op jit(solution)/shard_map/ppermute | solution.py:14
  55.0 0.6 fusion.39
  55.6 8.2 %collective-permute-done.2 = f32[128,1024]{1,0:T(8,128)S(1)} collective-permute-done((f32[128,1024]{1,0:T(8,128)S(1)}, f32[128,1024]{1,0:T(8,128)S(1)}, u32[]{:S(2)}, u32[]{:S(2)}) %collective-permute-start.2) | collective-permute-done | bytes 524320 | tf_op jit(solution)/shard_map/ppermute | solution.py:14
  64.3 40.4 %all-to-all-done.1 = bf16[4,384,1024]{2,1,0:T(8,128)(2,1)} async-done(((bf16[4,384,1024]{2,1,0:T(8,128)(2,1)}), bf16[4,384,1024]{2,1,0:T(8,128)(2,1)}, u32[]{:S(2)}, u32[]{:S(2)}) %all-to-all-start.1) | async-done | bytes 3145760 | tf_op jit(solution)/shard_map/all_to_all | solution.py:65
  104.7 8.3 %gather_fusion.1 = bf16[1024,1024]{1,0:T(8,128)(2,1)} fusion(bf16[1536,1024]{1,0:T(8,128)(2,1)} %bitcast.5, s32[1024]{0:T(1024)S(1)} %broadcast_clamp_fusion), kind=kCustom, calls=%fused_computation.1 | custom fusion | bytes 4198400 | tf_op jit(solution)/shard_map/gather | solution.py:66
  113.1 5.5 %fusion.7 = f32[128,1,8]{2,1,0:T(1,128)S(1)} fusion(bf16[1024,1024]{1,0:T(8,128)(2,1)} %gather_fusion.1, f32[128,1024,1]{1,0,2:T(8,128)S(1)} %bitcast.68), kind=kOutput, calls=%fused_computation.13 | convolution fusion | flops 12582912 | bytes 2625536 | tf_op jit(solution)/shard_map/rd,rkd->rk/dot_general | solution.py:69
  119.0 0.6 subtract_reduce_fusion
  119.8 7.9 %scatter_custom_fusion.1 = bf16[1536,1024]{1,0:T(8,128)(2,1)} fusion(s32[1024]{0:T(1024)} %bitcast.78, f32[128,1024]{1,0:T(8,128)S(1)} %copy-done.1, f32[1024]{0:T(1024)S(1)} %mul.127, bf16[]{:T(256)} %constant.61.clone.1), kind=kCustom, calls=%fused_computation.10 | custom fusion | flops 2097152 | bytes 3674624 | tf_op jit(solution)/shard_map/scatter | solution.py:103
  127.8 4.6 %all-to-all-start.2 = ((bf16[4,384,1024]{2,1,0:T(8,128)(2,1)}), bf16[4,384,1024]{2,1,0:T(8,128)(2,1)}, u32[]{:S(2)}, u32[]{:S(2)}) async-start(bf16[4,384,1024]{2,1,0:T(8,128)(2,1)} %bitcast.69), calls=%async_computation.2 | async-start | bytes 6291456 | tf_op jit(solution)/shard_map/all_to_all | solution.py:105
  133.1 9.5 %collective-permute-done.3 = f32[128,1024]{1,0:T(8,128)S(1)} collective-permute-done((f32[128,1024]{1,0:T(8,128)S(1)}, f32[128,1024]{1,0:T(8,128)S(1)}, u32[]{:S(2)}, u32[]{:S(2)}) %collective-permute-start.3) | collective-permute-done | bytes 524320 | tf_op jit(solution)/shard_map/ppermute | solution.py:14
  144.0 1.8 fusion.5
  145.8 7.1 %collective-permute-done.4 = f32[128,1024]{1,0:T(8,128)S(1)} collective-permute-done((f32[128,1024]{1,0:T(8,128)S(1)}, f32[128,1024]{1,0:T(8,128)S(1)}, u32[]{:S(2)}, u32[]{:S(2)}) %collective-permute-start.4) | collective-permute-done | bytes 524320 | tf_op jit(solution)/shard_map/ppermute | solution.py:14
  152.9 0.9 add.151
  153.8 1.5 convolution_add_fusion.4
  155.3 67.6 %psum.7 = f32[]{:T(128)} all-reduce(f32[]{:T(128)} %get-tuple-element.6), channel_id=1, replica_groups=mesh['blk'=8,'grp'=4] {'blk','grp'}, use_global_device_ids=true, to_apply=%region_16.17 | all-reduce | flops 1 | bytes 8 | tf_op jit(solution)/shard_map/psum | solution.py:86
  224.1 1.8 convolution_add_fusion.3
  226.0 1.1 add.152
  227.3 0.6 convolution_add_fusion.2
  228.0 1.5 fusion.14
  229.5 6.3 %collective-permute-done.6 = f32[128,1024]{1,0:T(8,128)S(1)} collective-permute-done((f32[128,1024]{1,0:T(8,128)S(1)}, f32[128,1024]{1,0:T(8,128)S(1)}, u32[]{:S(2)}, u32[]{:S(2)}) %collective-permute-start.6) | collective-permute-done | bytes 524320 | tf_op jit(solution)/shard_map/ppermute | solution.py:14
  235.8 0.9 multiply_subtract_fusion
  236.6 15.7 %scatter_custom_fusion.2 = f32[768,1024]{1,0:T(8,128)} fusion(s32[1536]{0:T(1024)S(1)} %fusion.31, bf16[1536,1024]{1,0:T(8,128)(2,1)} %bitcast.18, f32[]{:T(128)} %constant.59.clone.1), kind=kCustom, calls=%fused_computation.5 | custom fusion | flops 3145728 | bytes 6291460 | tf_op jit(solution)/shard_map/scatter-add | solution.py:107
  252.4 3.3 %convert_element_type.26 = bf16[768,1024]{1,0:T(8,128)(2,1)} convert(f32[768,1024]{1,0:T(8,128)} %scatter_custom_fusion.2) | non-fusion elementwise | flops 786432 | bytes 4718592 | tf_op jit(solution)/shard_map/convert_element_type | solution.py:110
  (66 shorter events, 7.3 us)
Async XLA Ops:
  0.6 20.5 %copy-start = (bf16[768,1024]{1,0:T(8,128)(2,1)S(1)}, bf16[768,1024]{1,0:T(8,128)(2,1)}, u32[]{:S(2)}) copy-start(bf16[768,1024]{1,0:T(8,128)(2,1)} %param.6) | copy-start | bytes 4718596
  5.0 39.7 %copy-start.7 = (s32[1024,1]{0,1:T(1,128)}, s32[1024,1]{0,1:T(1,128)S(1)}, u32[]{:S(2)}) copy-start(s32[1024,1]{0,1:T(1,128)S(1)} %compare_select_fusion.2) | copy-start | bytes 12292
  30.4 4.8 %copy-start.3 = (f32[128,1024]{1,0:T(8,128)S(1)}, f32[128,1024]{1,0:T(8,128)}, u32[]{:S(2)}) copy-start(f32[128,1024]{1,0:T(8,128)} %param.5) | copy-start | bytes 1572868
  30.4 14.4 %copy-start.1 = (f32[128,1024]{1,0:T(8,128)S(1)}, f32[128,1024]{1,0:T(8,128)}, u32[]{:S(2)}) copy-start(f32[128,1024]{1,0:T(8,128)} %param.4) | copy-start | bytes 1572868
  30.4 74.4 %all-to-all-start.1 = ((bf16[4,384,1024]{2,1,0:T(8,128)(2,1)}), bf16[4,384,1024]{2,1,0:T(8,128)(2,1)}, u32[]{:S(2)}, u32[]{:S(2)}) async-start(bf16[4,384,1024]{2,1,0:T(8,128)(2,1)} %broadcast_select_fusion), calls=%async_computation.1 | async-start | bytes 6291456 | tf_op jit(solution)/shard_map/all_to_all | solution.py:65
  35.2 9.6 %collective-permute-start = (f32[128,1024]{1,0:T(8,128)S(1)}, f32[128,1024]{1,0:T(8,128)S(1)}, u32[]{:S(2)}, u32[]{:S(2)}) collective-permute-start(f32[128,1024]{1,0:T(8,128)S(1)} %copy-done.3), channel_id=1, source_target_pairs={{0,4},{4,8},{8,12},{12,16},{16,20},{20,24},{24,28},{28,0},{1,5},{5... | collective-permute-start | bytes 1572872 | tf_op jit(solution)/shard_map/ppermute | solution.py:14
  44.7 19.0 %copy-start.6 = (f32[128,1024]{1,0:T(8,128)}, f32[128,1024]{1,0:T(8,128)S(1)}, u32[]{:S(2)}) copy-start(f32[128,1024]{1,0:T(8,128)S(1)} %collective-permute-done) | copy-start | bytes 1572868
  44.7 9.5 %collective-permute-start.1 = (f32[128,1024]{1,0:T(8,128)S(1)}, f32[128,1024]{1,0:T(8,128)S(1)}, u32[]{:S(2)}, u32[]{:S(2)}) collective-permute-start(f32[128,1024]{1,0:T(8,128)S(1)} %collective-permute-done), channel_id=1, source_target_pairs={{0,4},{4,8},{8,12},{12,16},{16,20},{20,24},{24,28},{28,0},{1,5},{5... | collective-permute-start | bytes 1572872 | tf_op jit(solution)/shard_map/ppermute | solution.py:14
  54.2 9.5 %copy-start.4 = (f32[128,1024]{1,0:T(8,128)}, f32[128,1024]{1,0:T(8,128)S(1)}, u32[]{:S(2)}) copy-start(f32[128,1024]{1,0:T(8,128)S(1)} %collective-permute-done.1) | copy-start | bytes 1572868
  54.2 9.5 %collective-permute-start.2 = (f32[128,1024]{1,0:T(8,128)S(1)}, f32[128,1024]{1,0:T(8,128)S(1)}, u32[]{:S(2)}, u32[]{:S(2)}) collective-permute-start(f32[128,1024]{1,0:T(8,128)S(1)} %collective-permute-done.1), channel_id=1, source_target_pairs={{0,4},{4,8},{8,12},{12,16},{16,20},{20,24},{24,28},{28,0},{1,5},{5... | collective-permute-start | bytes 1572872 | tf_op jit(solution)/shard_map/ppermute | solution.py:14
  127.8 108.9 %all-to-all-start.2 = ((bf16[4,384,1024]{2,1,0:T(8,128)(2,1)}), bf16[4,384,1024]{2,1,0:T(8,128)(2,1)}, u32[]{:S(2)}, u32[]{:S(2)}) async-start(bf16[4,384,1024]{2,1,0:T(8,128)(2,1)} %bitcast.69), calls=%async_computation.2 | async-start | bytes 6291456 | tf_op jit(solution)/shard_map/all_to_all | solution.py:105
  132.4 11.6 %copy-start.2 = (bf16[1024,1024]{1,0:T(8,128)(2,1)S(1)}, bf16[1024,1024]{1,0:T(8,128)(2,1)}, u32[]{:S(2)}) copy-start(bf16[1024,1024]{1,0:T(8,128)(2,1)} %gather_fusion.1) | copy-start | bytes 6291460
  133.0 9.6 %collective-permute-start.3 = (f32[128,1024]{1,0:T(8,128)S(1)}, f32[128,1024]{1,0:T(8,128)S(1)}, u32[]{:S(2)}, u32[]{:S(2)}) collective-permute-start(f32[128,1024]{1,0:T(8,128)S(1)} %fusion.16), channel_id=1, source_target_pairs={{0,4},{4,8},{8,12},{12,16},{16,20},{20,24},{24,28},{28,0},{1,5},{5... | collective-permute-start | bytes 1572872 | tf_op jit(solution)/shard_map/ppermute | solution.py:14
  143.1 9.8 %collective-permute-start.4 = (f32[128,1024]{1,0:T(8,128)S(1)}, f32[128,1024]{1,0:T(8,128)S(1)}, u32[]{:S(2)}, u32[]{:S(2)}) collective-permute-start(f32[128,1024]{1,0:T(8,128)S(1)} %convolution_add_fusion), channel_id=1, source_target_pairs={{0,4},{4,8},{8,12},{12,16},{16,20},{20,24},{24,28},{28,0},{1,5},{5... | collective-permute-start | bytes 1572872 | tf_op jit(solution)/shard_map/ppermute | solution.py:14
  153.8 72.2 %collective-permute-start.5 = (f32[128,1024]{1,0:T(8,128)}, f32[128,1024]{1,0:T(8,128)}, u32[]{:S(2)}, u32[]{:S(2)}) collective-permute-start(f32[128,1024]{1,0:T(8,128)} %add.151), channel_id=1, source_target_pairs={{0,4},{4,8},{8,12},{12,16},{16,20},{20,24},{24,28},{28,0},{1,5},{5... | collective-permute-start | bytes 1572872 | tf_op jit(solution)/shard_map/ppermute | solution.py:14
  223.5 3.8 %copy-start.5 = (f32[128,1024]{1,0:T(8,128)S(1)}, f32[128,1024]{1,0:T(8,128)}, u32[]{:S(2)}) copy-start(f32[128,1024]{1,0:T(8,128)} %copy-done.4) | copy-start | bytes 1572868
  227.1 8.7 %collective-permute-start.6 = (f32[128,1024]{1,0:T(8,128)S(1)}, f32[128,1024]{1,0:T(8,128)S(1)}, u32[]{:S(2)}, u32[]{:S(2)}) collective-permute-start(f32[128,1024]{1,0:T(8,128)S(1)} %add.152), channel_id=1, source_target_pairs={{0,20},{4,24},{8,28},{12,0},{16,4},{20,8},{24,12},{28,16},{1,21},{... | collective-permute-start | bytes 1572872 | tf_op jit(solution)/shard_map/ppermute | solution.py:14
where the time goes:
time: 262 us; the launch traced here: 257 us
  waiting for transfers between devices  89.8 us (34%)
  blocking collectives  79.3 us (30%)
  other arithmetic  37.5 us (14%)
  local copies, waits for them, and re-layouts  20 us (8%)
  matrix products  17.5 us (7%)
  starting transfers between devices  10 us (4%)
  between operations  2.72 us (1%)
    psum x1, blocking collectives, local(): total_loss = lax.psum(jnp.sum(lse - positive), ('blk', 'grp'))  67.6 us
    ppermute x7, waiting for transfers between devices, passed_along(): lax.ppermute(value, axis, [(i, (i + by) % length) for i in range(length)])  49.4 us
    all_to_all x1, waiting for transfers between devices, local(): lax.all_to_all(picked, 'grp', split_axis=0, concat_axis=0, tiled=True)  40.4 us
    scatter-add x1, other arithmetic, local(): table_accum.at[asked.reshape(-1)]  15.7 us
    all_to_all x1, blocking collectives, local(): lax.all_to_all(request, 'grp', split_axis=0, concat_axis=0, tiled=True)  11.7 us
    gather x1, local copies, waits for them, and re-layouts, local(): returned.reshape(group_count * capacity, feature_width)[slot_dest]  8.33 us
    scatter x1, other arithmetic, local(): outgoing.at[slot_dest]  7.95 us
    gather x1, local copies, waits for them, and re-layouts, local(): picked = jnp.take(hard_table, asked, axis=0)  5.84 us
  transfers between devices with their start and end apart: 9, of which 7 were waited for; matrix products, arithmetic and copies ran while one was open for 6% of the time, Pallas kernels for 0%

commit v1 on v0

v1 whole, which is shorter than its diff:
```python
import functools

import jax
import jax.numpy as jnp
from jax import lax
from jax.experimental import pallas as pl
from jax.experimental.pallas import tpu as pltpu
from jax.sharding import PartitionSpec as P

STOPS = 4
SCALE = 0.015625
TOP = 32766.0
LOW = -1e30
MESH = pl.DeviceIdType.MESH
HIGHEST = lax.Precision.HIGHEST

QUERY, QUERY_META, PASSAGE, PASSAGE_META, STATS, PARTIAL, LSE, GRAD = range(8)


def as_column(row, count):
    return jnp.broadcast_to(row, (128, count)).T[:, 0:1]


def as_row(column, count):
    return jnp.broadcast_to(column, (count, 128)).T[0:1, :]


def coded(value):
    largest = jnp.max(jnp.abs(value), axis=1, keepdims=True)
    largest = jnp.maximum(largest, 1e-30)
    code = jnp.round(value * (TOP / largest)).astype(jnp.int32).astype(jnp.int16)
    return code, largest * (1.0 / TOP)


def decoded(code):
    return code.astype(jnp.int32).astype(jnp.float32)


def nt(a, b, precision=None):
    return lax.dot_general(
        a, b, (((1,), (1,)), ((), ())), precision=precision, preferred_element_type=jnp.float32
    )


def kernel(
    loops, groups,
    q_ref, p_ref, t_ref, idx_ref,
    loss_ref, qg_ref, pg_ref, tg_ref,
    q16, qmeta, p16, pmeta, st_send, st_recv, a_send, a_recv, lse_send, lse_recv,
    g_send, g_recv, l_send, l_recv, sh, ch, sw, pf, qhi, qlo, whi,
    send_sem, recv_sem, lsend_sem, lrecv_sem,
):
    b = lax.axis_index("blk")
    g = lax.axis_index("grp")
    rows, width = q_ref.shape
    table_rows = t_ref.shape[0]
    barrier = pltpu.get_barrier_semaphore()
    for j in range(1, groups):
        pl.semaphore_signal(
            barrier, inc=1, device_id=(b, lax.rem(g + j, groups)), device_id_type=MESH
        )

    def greet(k, carry):
        pl.semaphore_signal(
            barrier, inc=1, device_id=(lax.rem(b + k, loops), g), device_id_type=MESH
        )
        return carry

    lax.fori_loop(1, loops, greet, 0)

    def copy(kind, j, src, dst, device):
        return pltpu.make_async_remote_copy(
            src_ref=src,
            dst_ref=dst,
            send_sem=send_sem.at[kind, j],
            recv_sem=recv_sem.at[kind, j],
            device_id=device,
            device_id_type=MESH,
        )

    def ahead(j):
        return (b, lax.rem(g + j, groups))

    def behind(j):
        return (b, lax.rem(g + groups - j, groups))

    copies = {}

    def go(kind, j, src, dst, device):
        copies[kind, j] = copy(kind, j, src, dst, device)
        copies[kind, j].start()

    query = q_ref[...]
    code, scale = coded(query)
    q16[0] = code
    qmeta[0, 0:8, :] = idx_ref[...]
    qmeta[0, 8:16, :] = jnp.broadcast_to(as_row(scale, rows), (8, rows))
    code, scale = coded(p_ref[...])
    p16[0] = code
    pmeta[0] = jnp.broadcast_to(as_row(scale, rows), (8, rows))

    pl.semaphore_wait(barrier, groups - 1 + loops - 1)
    for j in range(1, groups):
        go(QUERY_META, j, qmeta.at[0], qmeta.at[j], ahead(j))
    for s in range(1, STOPS):
        go(PASSAGE_META, s, pmeta.at[0], pmeta.at[s], (lax.rem(b + s, loops), g))
    for j in range(1, groups):
        go(QUERY, j, q16.at[0], q16.at[j], ahead(j))
    for s in range(1, STOPS):
        go(PASSAGE, s, p16.at[0], p16.at[s], (lax.rem(b + s, loops), g))

    row_id = lax.broadcasted_iota(jnp.int32, (table_rows, rows), 0).astype(jnp.float32) + (
        g * table_rows
    ).astype(jnp.float32)

    def hard_part(j):
        value = decoded(q16[j])
        high = value.astype(jnp.bfloat16)
        low = (value - high.astype(jnp.float32)).astype(jnp.bfloat16)
        qhi[j * rows:(j + 1) * rows, :] = high
        qlo[j * rows:(j + 1) * rows, :] = low
        table = t_ref[...]
        scores = (nt(table, high) + nt(table, low)) * (qmeta[j, 8:9, :] * SCALE)
        named = jnp.zeros((table_rows, rows), jnp.float32)
        for k in range(8):
            named = named + jnp.where(row_id == qmeta[j, k:k + 1, :], 1.0, 0.0)
        top = jnp.max(jnp.where(named > 0.0, scores, LOW), axis=0, keepdims=True)
        part = jnp.where(named > 0.0, named * jnp.exp(jnp.minimum(scores - top, 0.0)), 0.0)
        sh[j] = scores
        ch[j] = named
        st_send[j, 0:1, :] = top
        st_send[j, 1:2, :] = jnp.sum(part, axis=0, keepdims=True)
        if j > 0:
            go(STATS, j, st_send.at[j], st_recv.at[j], behind(j))
        partial = jnp.dot(
            part.T.astype(jnp.bfloat16), table, preferred_element_type=jnp.float32
        )
        a_send[j] = partial.astype(jnp.bfloat16)
        if j > 0:
            go(PARTIAL, j, a_send.at[j], a_recv.at[j], behind(j))

    def window_part(s):
        if s == 0:
            block = p_ref[...]
        else:
            block = decoded(p16[s]) * as_column(pmeta[s, 0:1, :], rows)
        pf[s * rows:(s + 1) * rows, :] = block
        sw[s * rows:(s + 1) * rows, :] = nt(block, query, HIGHEST) * SCALE

    st_send[...] = jnp.zeros_like(st_send)
    hard_part(0)
    window_part(0)
    positive = jnp.sum(query * p_ref[...]) * SCALE
    for s in range(1, STOPS):
        copies[PASSAGE_META, s].wait_recv()
        copies[PASSAGE, s].wait_recv()
        window_part(s)
    for j in range(1, groups):
        copies[QUERY_META, j].wait_recv()
        copies[QUERY, j].wait_recv()
        hard_part(j)

    window = sw[...]
    tops = [jnp.max(window, axis=0, keepdims=True), st_send[0, 0:1, :]]
    for j in range(1, groups):
        copies[STATS, j].wait_recv()
        tops.append(st_recv[j, 0:1, :])
    top = functools.reduce(jnp.maximum, tops)
    total = jnp.sum(jnp.exp(window - top), axis=0, keepdims=True)
    total = total + st_send[0, 1:2, :] * jnp.exp(tops[1] - top)
    for j in range(1, groups):
        total = total + st_recv[j, 1:2, :] * jnp.exp(tops[j + 1] - top)
    lse = top + jnp.log(total)
    lse_send[0:1, :] = lse
    lse_send[1:8, :] = jnp.broadcast_to(jnp.sum(lse) - positive, (7, rows))
    for j in range(1, groups):
        go(LSE, j, lse_send, lse_recv.at[j], ahead(j))

    weight = jnp.exp(window - lse)
    sw[...] = weight
    for s in range(STOPS - 1, 0, -1):
        term = jnp.dot(
            sw[s * rows:(s + 1) * rows, :], query,
            precision=HIGHEST, preferred_element_type=jnp.float32,
        )
        g_send[s] = term.astype(jnp.bfloat16)
        go(GRAD, s, g_send.at[s], g_recv.at[s], (lax.rem(b + loops - s, loops), g))

    group_loss = lse_send[1:2, :]
    whi[:, 0:rows] = (
        ch[0] * jnp.exp(jnp.minimum(sh[0] - lse, 0.0)) * (qmeta[0, 8:9, :] * SCALE)
    ).astype(jnp.bfloat16)
    for j in range(1, groups):
        copies[LSE, j].wait_recv()
        group_loss = group_loss + lse_recv[j, 1:2, :]
        whi[:, j * rows:(j + 1) * rows] = jnp.where(
            ch[j] > 0.0,
            ch[j] * jnp.exp(jnp.minimum(sh[j] - lse_recv[j, 0:1, :], 0.0)) * (qmeta[j, 8:9, :] * SCALE),
            0.0,
        ).astype(jnp.bfloat16)

    l_send[...] = jnp.broadcast_to(group_loss, (8, rows))
    l_recv[0] = jnp.broadcast_to(group_loss, (8, rows))

    def loss_copy(k):
        return pltpu.make_async_remote_copy(
            src_ref=l_send,
            dst_ref=l_recv.at[k],
            send_sem=lsend_sem.at[k],
            recv_sem=lrecv_sem.at[k],
            device_id=(lax.rem(b + k, loops), g),
            device_id_type=MESH,
        )

    def loss_start(k, carry):
        loss_copy(k).start()
        return carry

    lax.fori_loop(1, loops, loss_start, 0)

    tile = 256

    def table_tile(step, carry):
        cols = pl.ds(pl.multiple_of(step * tile, tile), tile)
        left = whi[...]
        tg_ref[:, cols] = (
            jnp.dot(left, qhi[:, cols], preferred_element_type=jnp.float32)
            + jnp.dot(left, qlo[:, cols], preferred_element_type=jnp.float32)
        ).astype(jnp.bfloat16)
        return carry

    lax.fori_loop(0, width // tile, table_tile, 0)

    qg_ref[...] = jnp.dot(
        sw[...].T, pf[...], precision=HIGHEST, preferred_element_type=jnp.float32
    )
    pg_ref[...] = jnp.dot(
        sw[0:rows, :], query, precision=HIGHEST, preferred_element_type=jnp.float32
    )

    parts = a_send[0].astype(jnp.float32) * as_column(jnp.exp(tops[1] - lse), rows)
    for j in range(1, groups):
        copies[PARTIAL, j].wait_recv()
        parts = parts + a_recv[j].astype(jnp.float32) * as_column(jnp.exp(tops[j + 1] - lse), rows)
    qg_ref[...] = (qg_ref[...] + parts - p_ref[...]) * SCALE
    sums = pg_ref[...]
    for s in range(1, STOPS):
        copies[GRAD, s].wait_recv()
        sums = sums + g_recv[s].astype(jnp.float32)
    pg_ref[...] = (sums - query) * SCALE

    def loss_wait(k, carry):
        loss_copy(k).wait()
        return carry

    lax.fori_loop(1, loops, loss_wait, 0)
    loss_ref[0, 0] = jnp.sum(l_recv[:, 0:1, 0:1]) / (rows * loops * groups)
    for each in copies.values():
        each.wait_send()


def local(loops, groups, queries, passages, hard_table, hard_index):
    rows, width = queries.shape
    table_rows = hard_table.shape[0]
    index = hard_index.T.astype(jnp.float32)
    vmem = pl.BlockSpec(memory_space=pltpu.VMEM)
    f32, bf16, i16 = jnp.float32, jnp.bfloat16, jnp.int16
    out = pl.pallas_call(
        functools.partial(kernel, loops, groups),
        out_shape=(
            jax.ShapeDtypeStruct((1, 1), f32),
            jax.ShapeDtypeStruct((rows, width), f32),
            jax.ShapeDtypeStruct((rows, width), f32),
            jax.ShapeDtypeStruct((table_rows, width), bf16),
        ),
        in_specs=[vmem] * 4,
        out_specs=(pl.BlockSpec(memory_space=pltpu.SMEM), vmem, vmem, vmem),
        scratch_shapes=[
            pltpu.VMEM((groups, rows, width), i16),
            pltpu.VMEM((groups, 16, rows), f32),
            pltpu.VMEM((STOPS, rows, width), i16),
            pltpu.VMEM((STOPS, 8, rows), f32),
            pltpu.VMEM((groups, 8, rows), f32),
            pltpu.VMEM((groups, 8, rows), f32),
            pltpu.VMEM((groups, rows, width), bf16),
            pltpu.VMEM((groups, rows, width), bf16),
            pltpu.VMEM((8, rows), f32),
            pltpu.VMEM((groups, 8, rows), f32),
            pltpu.VMEM((STOPS, rows, width), bf16),
            pltpu.VMEM((STOPS, rows, width), bf16),
            pltpu.VMEM((8, rows), f32),
            pltpu.VMEM((loops, 8, rows), f32),
            pltpu.VMEM((groups, table_rows, rows), f32),
            pltpu.VMEM((groups, table_rows, rows), f32),
            pltpu.VMEM((STOPS * rows, rows), f32),
            pltpu.VMEM((STOPS * rows, width), f32),
            pltpu.VMEM((groups * rows, width), bf16),
            pltpu.VMEM((groups * rows, width), bf16),
            pltpu.VMEM((table_rows, groups * rows), bf16),
            pltpu.SemaphoreType.DMA((8, max(groups, STOPS))),
            pltpu.SemaphoreType.DMA((8, max(groups, STOPS))),
            pltpu.SemaphoreType.DMA((loops,)),
            pltpu.SemaphoreType.DMA((loops,)),
        ],
        compiler_params=pltpu.CompilerParams(
            collective_id=0, has_side_effects=True, vmem_limit_bytes=48 * 1024 * 1024
        ),
    )(queries, passages, hard_table, index)
    return (out[0].reshape(()), out[1], out[2], out[3])


def solution(mesh):
    rows = P(("blk", "grp"), None)
    return jax.shard_map(
        functools.partial(local, mesh.shape["blk"], mesh.shape["grp"]),
        mesh=mesh,
        in_specs=(rows, rows, rows, rows),
        out_specs=(P(), rows, rows, rows),
        check_vma=False,
    )
```

time: 262 us -> 76.7 us (0.29); the launches traced: 257 us -> 76 us
  waiting for transfers between devices: 89.8 us -> 0 us
  blocking collectives: 79.3 us -> 0 us
  Pallas kernels: 0 us -> 66.7 us
  other arithmetic: 37.5 us -> 0.69 us
  matrix products: 17.5 us -> 0 us
  local copies, waits for them, and re-layouts: 20 us -> 6.22 us
  starting transfers between devices: 10 us -> 0 us
    psum x1 -> x0, blocking collectives: 67.6 us -> none  [local(): total_loss = lax.psum(jnp.sum(lse - positive), ('blk', 'grp'))]
    pallas_call x0 -> x1, Pallas kernels: none -> 66.7 us  [local(): pl.pallas_call(functools.partial(kernel, loops, groups), out_shape=(jax.S...]
    ppermute x7 -> x0, waiting for transfers between devices: 49.4 us -> none  [passed_along(): lax.ppermute(value, axis, [(i, (i + by) % length) for i in range(length)])]
    all_to_all x2 -> x0, waiting for transfers between devices: 40.4 us -> none  [the longest x1 40.4 us: local(): lax.all_to_all(picked, 'grp', split_axis=0, concat_axis=0, tiled=True)]
    dot_general x14 -> x0, matrix products: 17.5 us -> none  [the longest x1 5.51 us: local(): jnp.einsum('rd,rkd->rk', queries, hard_vecs, precision=lax.Precision.HIGH...]
    scatter-add x1 -> x0, other arithmetic: 15.7 us -> none  [local(): table_accum.at[asked.reshape(-1)]]
    gather x2 -> x0, local copies, waits for them, and re-layouts: 14.2 us -> none  [the longest x1 8.33 us: local(): returned.reshape(group_count * capacity, feature_width)[slot_dest]]
    all_to_all x1 -> x0, blocking collectives: 11.7 us -> none  [local(): lax.all_to_all(request, 'grp', split_axis=0, concat_axis=0, tiled=True)]
  transfers between devices with their start and end apart: 9 -> 0, of which waited for: 7 -> 0; matrix products, arithmetic and copies ran while one was open for 6% -> 0% of each run, Pallas kernels for 0% -> 0%
where the time goes in v1:
time: 76.7 us; the launch traced here: 76 us
  Pallas kernels  66.7 us (87%)
  local copies, waits for them, and re-layouts  6.22 us (8%)
  between operations  2.38 us (3%)
    pallas_call x1, Pallas kernels, local(): pl.pallas_call(functools.partial(kernel, loops, groups), out_shape=(jax.S...  66.7 us
    unnamed x9, local copies, waits for them, and re-layouts  6.22 us

profile of v1, /device:TPU:0, one launch (start us, length us, event | category | flops | bytes accessed | tf_op | source)
XLA Modules:
  0.0 76.0 jit_solution(1758777929490861390)
XLA Ops:
  0.6 0.7 convert_bitcast_fusion.idx_ref
  1.3 0.0 copy-start
  1.3 1.4 %copy-done = bf16[768,1024]{1,0:T(8,128)(2,1)S(1)} copy-done((bf16[768,1024]{1,0:T(8,128)(2,1)S(1)}, bf16[768,1024]{1,0:T(8,128)(2,1)}, u32[]{:S(2)}) %copy-start) | copy-done | bytes 1572888
  2.7 0.0 copy-start.1
  2.7 1.0 %copy-done.1 = f32[128,1024]{1,0:T(8,128)S(1)} copy-done((f32[128,1024]{1,0:T(8,128)S(1)}, f32[128,1024]{1,0:T(8,128)}, u32[]{:S(2)}) %copy-start.1) | copy-done | bytes 524312
  3.8 0.0 copy-start.2
  3.8 1.0 %copy-done.2 = f32[128,1024]{1,0:T(8,128)S(1)} copy-done((f32[128,1024]{1,0:T(8,128)S(1)}, f32[128,1024]{1,0:T(8,128)}, u32[]{:S(2)}) %copy-start.2) | copy-done | bytes 524312
  4.8 66.7 %shard_map.75 = (f32[1,1]{1,0:T(1,128)}, f32[128,1024]{1,0:T(8,128)S(1)}, f32[128,1024]{1,0:T(8,128)S(1)}, bf16[768,1024]{1,0:T(8,128)(2,1)S(1)}) custom-call(f32[128,1024]{1,0:T(8,128)S(1)} %copy-done.1, f32[128,1024]{1,0:T(8,128)S(1)} %copy-done.2, bf16[768,1024]{1,0:T(8,128)(2,1)S(1)} %copy-done, f32[8,128]{1,0:T(8,128)S(1)} %convert_bitcast_fusion.idx_ref), custom_call_target="tpu_custom_call" | custom-call | tf_op jit(solution)/shard_map/pallas_call | solution.py:268
  72.2 0.8 %copy.13 = f32[128,1024]{1,0:T(8,128)} copy(f32[128,1024]{1,0:T(8,128)S(1)} %get-tuple-element.17) | data formatting | bytes 1048576
  73.0 0.8 %copy.14 = f32[128,1024]{1,0:T(8,128)} copy(f32[128,1024]{1,0:T(8,128)S(1)} %get-tuple-element.18) | data formatting | bytes 1048576
  73.8 1.1 %copy.15 = bf16[768,1024]{1,0:T(8,128)(2,1)} copy(bf16[768,1024]{1,0:T(8,128)(2,1)S(1)} %get-tuple-element.19) | data formatting | bytes 3145728
Async XLA Ops:
  1.3 1.4 %copy-start = (bf16[768,1024]{1,0:T(8,128)(2,1)S(1)}, bf16[768,1024]{1,0:T(8,128)(2,1)}, u32[]{:S(2)}) copy-start(bf16[768,1024]{1,0:T(8,128)(2,1)} %t_ref.1) | copy-start | bytes 4718596
  2.7 1.0 %copy-start.1 = (f32[128,1024]{1,0:T(8,128)S(1)}, f32[128,1024]{1,0:T(8,128)}, u32[]{:S(2)}) copy-start(f32[128,1024]{1,0:T(8,128)} %q_ref.1) | copy-start | bytes 1572868
  3.8 1.0 %copy-start.2 = (f32[128,1024]{1,0:T(8,128)S(1)}, f32[128,1024]{1,0:T(8,128)}, u32[]{:S(2)}) copy-start(f32[128,1024]{1,0:T(8,128)} %p_ref.1) | copy-start | bytes 1572868

commit v2 on v1

--- a/solution.py
+++ b/solution.py
@@ -44,16 +44,22 @@
 
 def kernel(
     loops, groups,
-    q_ref, p_ref, t_ref, idx_ref,
+    q_hbm, p_hbm, t_hbm, idx_ref,
     loss_ref, qg_ref, pg_ref, tg_ref,
-    q16, qmeta, p16, pmeta, st_send, st_recv, a_send, a_recv, lse_send, lse_recv,
+    q_ref, p_ref, t_ref, q16, qmeta, p16, pmeta, st_send, st_recv, a_send, a_recv, lse_send, lse_recv,
     g_send, g_recv, l_send, l_recv, sh, ch, sw, pf, qhi, qlo, whi,
-    send_sem, recv_sem, lsend_sem, lrecv_sem,
+    send_sem, recv_sem, lsend_sem, lrecv_sem, load_sem,
 ):
     b = lax.axis_index("blk")
     g = lax.axis_index("grp")
     rows, width = q_ref.shape
     table_rows = t_ref.shape[0]
+    loads = [
+        pltpu.make_async_copy(src, dst, load_sem.at[i])
+        for i, (src, dst) in enumerate(((q_hbm, q_ref), (p_hbm, p_ref), (t_hbm, t_ref)))
+    ]
+    for load in loads:
+        load.start()
     barrier = pltpu.get_barrier_semaphore()
     for j in range(1, groups):
         pl.semaphore_signal(
@@ -68,62 +74,98 @@
 
     lax.fori_loop(1, loops, greet, 0)
 
-    def copy(kind, j, src, dst, device):
+    def copy(kind, j, src, dst, device, slot=None):
         return pltpu.make_async_remote_copy(
             src_ref=src,
             dst_ref=dst,
             send_sem=send_sem.at[kind, j],
-            recv_sem=recv_sem.at[kind, j],
+            recv_sem=recv_sem.at[kind, j if slot is None else slot],
             device_id=device,
             device_id_type=MESH,
         )
 
-    def ahead(j):
-        return (b, lax.rem(g + j, groups))
-
-    def behind(j):
-        return (b, lax.rem(g + groups - j, groups))
-
     copies = {}
 
-    def go(kind, j, src, dst, device):
-        copies[kind, j] = copy(kind, j, src, dst, device)
+    def go(kind, j, src, dst, device, slot=None):
+        copies[kind, j] = copy(kind, j, src, dst, device, slot)
         copies[kind, j].start()
 
+    def arrived(kind, slot, ref):
+        copy(kind, 0, ref, ref, (b, lax.rem(g + 1, groups)), slot).wait_recv()
+
+    near = jnp.minimum(g, groups - 1 - g)
+    right_longer = (g < groups - 1 - g).astype(jnp.int32)
+    others = [None]
+    for i in range(groups - 1):
+        both = (i < 2 * near).astype(jnp.int32)
+        distance = both * (i // 2 + 1) + (1 - both) * (i - near + 1)
+        right = both * (i % 2) + (1 - both) * right_longer
+        others.append(g + distance * (2 * right - 1))
+
+    own_right = copy(QUERY, 0, q16.at[g], q16.at[g], (b, jnp.minimum(g + 1, groups - 1)), g)
+    own_left = copy(QUERY, groups, q16.at[g], q16.at[g], (b, jnp.maximum(g - 1, 0)), g)
+
+    def onward(j):
+        src = others[j]
+        step = jnp.where(src < g, 1, -1)
+        dst = g + step
+        return (dst >= 0) & (dst < groups), copy(
+            QUERY, j, q16.at[src], q16.at[src], (b, jnp.clip(dst, 0, groups - 1)), src
+        )
+
+    def receive(j):
+        src = others[j]
+        arrived(QUERY, src, q16.at[src])
+        valid, forward = onward(j)
+
+        @pl.when(valid)
+        def _():
+            forward.start()
+
+    loads[0].wait()
     query = q_ref[...]
     code, scale = coded(query)
-    q16[0] = code
-    qmeta[0, 0:8, :] = idx_ref[...]
-    qmeta[0, 8:16, :] = jnp.broadcast_to(as_row(scale, rows), (8, rows))
+    q16[g] = code
+    qmeta[g, 0:8, :] = idx_ref[...]
+    qmeta[g, 8:16, :] = jnp.broadcast_to(as_row(scale, rows), (8, rows))
+    pl.semaphore_wait(barrier, groups - 1 + loops - 1)
+
+    @pl.when(g < groups - 1)
+    def _():
+        own_right.start()
+
+    @pl.when(g > 0)
+    def _():
+        own_left.start()
+
+    for j in range(1, groups):
+        go(QUERY_META, j, qmeta.at[g], qmeta.at[g], (b, others[j]), g)
+    loads[1].wait()
     code, scale = coded(p_ref[...])
     p16[0] = code
     pmeta[0] = jnp.broadcast_to(as_row(scale, rows), (8, rows))
-
-    pl.semaphore_wait(barrier, groups - 1 + loops - 1)
-    for j in range(1, groups):
-        go(QUERY_META, j, qmeta.at[0], qmeta.at[j], ahead(j))
     for s in range(1, STOPS):
         go(PASSAGE_META, s, pmeta.at[0], pmeta.at[s], (lax.rem(b + s, loops), g))
-    for j in range(1, groups):
-        go(QUERY, j, q16.at[0], q16.at[j], ahead(j))
     for s in range(1, STOPS):
         go(PASSAGE, s, p16.at[0], p16.at[s], (lax.rem(b + s, loops), g))
+    loads[2].wait()
 
     row_id = lax.broadcasted_iota(jnp.int32, (table_rows, rows), 0).astype(jnp.float32) + (
         g * table_rows
     ).astype(jnp.float32)
 
     def hard_part(j):
-        value = decoded(q16[j])
+        src = g if j == 0 else others[j]
+        value = decoded(q16[src])
         high = value.astype(jnp.bfloat16)
         low = (value - high.astype(jnp.float32)).astype(jnp.bfloat16)
         qhi[j * rows:(j + 1) * rows, :] = high
         qlo[j * rows:(j + 1) * rows, :] = low
         table = t_ref[...]
-        scores = (nt(table, high) + nt(table, low)) * (qmeta[j, 8:9, :] * SCALE)
+        scores = (nt(table, high) + nt(table, low)) * (qmeta[src, 8:9, :] * SCALE)
         named = jnp.zeros((table_rows, rows), jnp.float32)
         for k in range(8):
-            named = named + jnp.where(row_id == qmeta[j, k:k + 1, :], 1.0, 0.0)
+            named = named + jnp.where(row_id == qmeta[src, k:k + 1, :], 1.0, 0.0)
         top = jnp.max(jnp.where(named > 0.0, scores, LOW), axis=0, keepdims=True)
         part = jnp.where(named > 0.0, named * jnp.exp(jnp.minimum(scores - top, 0.0)), 0.0)
         sh[j] = scores
@@ -131,13 +173,13 @@
         st_send[j, 0:1, :] = top
         st_send[j, 1:2, :] = jnp.sum(part, axis=0, keepdims=True)
         if j > 0:
-            go(STATS, j, st_send.at[j], st_recv.at[j], behind(j))
+            go(STATS, j, st_send.at[j], st_recv.at[g], (b, src), g)
         partial = jnp.dot(
             part.T.astype(jnp.bfloat16), table, preferred_element_type=jnp.float32
         )
         a_send[j] = partial.astype(jnp.bfloat16)
         if j > 0:
-            go(PARTIAL, j, a_send.at[j], a_recv.at[j], behind(j))
+            go(PARTIAL, j, a_send.at[j], a_recv.at[g], (b, src), g)
 
     def window_part(s):
         if s == 0:
@@ -151,30 +193,50 @@
     hard_part(0)
     window_part(0)
     positive = jnp.sum(query * p_ref[...]) * SCALE
-    for s in range(1, STOPS):
+    def window_next(s):
         copies[PASSAGE_META, s].wait_recv()
         copies[PASSAGE, s].wait_recv()
         window_part(s)
-    for j in range(1, groups):
-        copies[QUERY_META, j].wait_recv()
-        copies[QUERY, j].wait_recv()
+
+    receive(1)
+    if groups > 2:
+
+        @pl.when(near > 0)
+        def _():
+            receive(2)
+
+    arrived(QUERY_META, others[1], qmeta.at[others[1]])
+    hard_part(1)
+    if groups > 2:
+
+        @pl.when(near == 0)
+        def _():
+            receive(2)
+
+    window_next(1)
+    for j in range(2, groups):
+        if j > 2:
+            receive(j)
+        arrived(QUERY_META, others[j], qmeta.at[others[j]])
         hard_part(j)
+    for s in range(2, STOPS):
+        window_next(s)
 
     window = sw[...]
     tops = [jnp.max(window, axis=0, keepdims=True), st_send[0, 0:1, :]]
     for j in range(1, groups):
-        copies[STATS, j].wait_recv()
-        tops.append(st_recv[j, 0:1, :])
+        arrived(STATS, others[j], st_recv.at[others[j]])
+        tops.append(st_recv[others[j], 0:1, :])
     top = functools.reduce(jnp.maximum, tops)
     total = jnp.sum(jnp.exp(window - top), axis=0, keepdims=True)
     total = total + st_send[0, 1:2, :] * jnp.exp(tops[1] - top)
     for j in range(1, groups):
-        total = total + st_recv[j, 1:2, :] * jnp.exp(tops[j + 1] - top)
+        total = total + st_recv[others[j], 1:2, :] * jnp.exp(tops[j + 1] - top)
     lse = top + jnp.log(total)
     lse_send[0:1, :] = lse
     lse_send[1:8, :] = jnp.broadcast_to(jnp.sum(lse) - positive, (7, rows))
     for j in range(1, groups):
-        go(LSE, j, lse_send, lse_recv.at[j], ahead(j))
+        go(LSE, j, lse_send, lse_recv.at[g], (b, others[j]), g)
 
     weight = jnp.exp(window - lse)
     sw[...] = weight
@@ -188,14 +250,14 @@
 
     group_loss = lse_send[1:2, :]
     whi[:, 0:rows] = (
-        ch[0] * jnp.exp(jnp.minimum(sh[0] - lse, 0.0)) * (qmeta[0, 8:9, :] * SCALE)
+        ch[0] * jnp.exp(jnp.minimum(sh[0] - lse, 0.0)) * (qmeta[g, 8:9, :] * SCALE)
     ).astype(jnp.bfloat16)
     for j in range(1, groups):
-        copies[LSE, j].wait_recv()
-        group_loss = group_loss + lse_recv[j, 1:2, :]
+        arrived(LSE, others[j], lse_recv.at[others[j]])
+        group_loss = group_loss + lse_recv[others[j], 1:2, :]
         whi[:, j * rows:(j + 1) * rows] = jnp.where(
             ch[j] > 0.0,
-            ch[j] * jnp.exp(jnp.minimum(sh[j] - lse_recv[j, 0:1, :], 0.0)) * (qmeta[j, 8:9, :] * SCALE),
+            ch[j] * jnp.exp(jnp.minimum(sh[j] - lse_recv[others[j], 0:1, :], 0.0)) * (qmeta[others[j], 8:9, :] * SCALE),
             0.0,
         ).astype(jnp.bfloat16)
 
@@ -240,8 +302,8 @@
 
     parts = a_send[0].astype(jnp.float32) * as_column(jnp.exp(tops[1] - lse), rows)
     for j in range(1, groups):
-        copies[PARTIAL, j].wait_recv()
-        parts = parts + a_recv[j].astype(jnp.float32) * as_column(jnp.exp(tops[j + 1] - lse), rows)
+        arrived(PARTIAL, others[j], a_recv.at[others[j]])
+        parts = parts + a_recv[others[j]].astype(jnp.float32) * as_column(jnp.exp(tops[j + 1] - lse), rows)
     qg_ref[...] = (qg_ref[...] + parts - p_ref[...]) * SCALE
     sums = pg_ref[...]
     for s in range(1, STOPS):
@@ -257,6 +319,21 @@
     loss_ref[0, 0] = jnp.sum(l_recv[:, 0:1, 0:1]) / (rows * loops * groups)
     for each in copies.values():
         each.wait_send()
+
+    @pl.when(g < groups - 1)
+    def _():
+        own_right.wait_send()
+
+    @pl.when(g > 0)
+    def _():
+        own_left.wait_send()
+
+    for j in range(1, groups):
+        valid, forward = onward(j)
+
+        @pl.when(valid)
+        def _():
+            forward.wait_send()
 
 
 def local(loops, groups, queries, passages, hard_table, hard_index):
@@ -273,9 +350,12 @@
             jax.ShapeDtypeStruct((rows, width), f32),
             jax.ShapeDtypeStruct((table_rows, width), bf16),
         ),
-        in_specs=[vmem] * 4,
+        in_specs=[pl.BlockSpec(memory_space=pl.ANY)] * 3 + [vmem],
         out_specs=(pl.BlockSpec(memory_space=pltpu.SMEM), vmem, vmem, vmem),
         scratch_shapes=[
+            pltpu.VMEM((rows, width), f32),
+            pltpu.VMEM((rows, width), f32),
+            pltpu.VMEM((table_rows, width), bf16),
             pltpu.VMEM((groups, rows, width), i16),
             pltpu.VMEM((groups, 16, rows), f32),
             pltpu.VMEM((STOPS, rows, width), i16),
@@ -297,13 +377,14 @@
             pltpu.VMEM((groups * rows, width), bf16),
             pltpu.VMEM((groups * rows, width), bf16),
             pltpu.VMEM((table_rows, groups * rows), bf16),
-            pltpu.SemaphoreType.DMA((8, max(groups, STOPS))),
-            pltpu.SemaphoreType.DMA((8, max(groups, STOPS))),
+            pltpu.SemaphoreType.DMA((8, max(groups, STOPS) + 1)),
+            pltpu.SemaphoreType.DMA((8, max(groups, STOPS) + 1)),
             pltpu.SemaphoreType.DMA((loops,)),
             pltpu.SemaphoreType.DMA((loops,)),
+            pltpu.SemaphoreType.DMA((3,)),
         ],
         compiler_params=pltpu.CompilerParams(
-            collective_id=0, has_side_effects=True, vmem_limit_bytes=48 * 1024 * 1024
+            collective_id=0, has_side_effects=True, vmem_limit_bytes=60 * 1024 * 1024
         ),
     )(queries, passages, hard_table, index)
     return (out[0].reshape(()), out[1], out[2], out[3])

time: 76.7 us -> 67.5 us (0.88)
  Pallas kernels: 66.7 us -> 57.6 us
  local copies, waits for them, and re-layouts: 6.22 us -> 4.92 us
    pallas_call x1, Pallas kernels: 66.7 us -> 57.6 us  [local(): pl.pallas_call(functools.partial(kernel, loops, groups), out_shape=(jax.S...]
    unnamed x9 -> x5, local copies, waits for them, and re-layouts: 6.22 us -> 4.92 us
where the time goes in v2:
time: 67.5 us; the launch traced here: 66.3 us
  Pallas kernels  57.6 us (85%)
  local copies, waits for them, and re-layouts  4.92 us (7%)
  between operations  2.46 us (4%)
  other arithmetic  1.28 us (2%)
    pallas_call x1, Pallas kernels, local(): pl.pallas_call(functools.partial(kernel, loops, groups), out_shape=(jax.S...  57.6 us
    unnamed x5, local copies, waits for them, and re-layouts  4.92 us

profile of v2, /device:TPU:0, one launch (start us, length us, event | category | flops | bytes accessed | tf_op | source)
XLA Modules:
  0.0 66.3 jit_solution(6719951890963706265)
XLA Ops:
  0.6 1.3 %convert_bitcast_fusion.idx_ref = f32[8,128]{1,0:T(8,128)} fusion(s32[128,8]{0,1:T(8,128)} %param.7), kind=kLoop, calls=%fused_computation | loop fusion | flops 1024 | bytes 8192 | tf_op jit(solution)/shard_map/convert_element_type | solution.py:342
  1.9 57.6 %shard_map.75 = (f32[1,1]{1,0:T(1,128)}, f32[128,1024]{1,0:T(8,128)}, f32[128,1024]{1,0:T(8,128)}, bf16[768,1024]{1,0:T(8,128)(2,1)}) custom-call(f32[128,1024]{1,0:T(8,128)} %q_hbm.1, f32[128,1024]{1,0:T(8,128)} %p_hbm.1, bf16[768,1024]{1,0:T(8,128)(2,1)} %t_hbm.1, f32[8,128]{1,0:T(8,128)} %convert_bitcast_fusion.idx_ref), custom_call_target="tpu_custom_call" | custom-call | tf_op jit(solution)/shard_map/pallas_call | solution.py:345
  59.6 0.0 copy-start
  60.2 1.9 %copy.13 = f32[128,1024]{1,0:T(8,128)} copy(f32[128,1024]{1,0:T(8,128)} %get-tuple-element.17) | data formatting | bytes 1048576
  62.1 1.9 %copy.14 = f32[128,1024]{1,0:T(8,128)} copy(f32[128,1024]{1,0:T(8,128)} %get-tuple-element.18) | data formatting | bytes 1048576
  64.0 0.0 copy-done
  64.0 1.1 %copy.15 = bf16[768,1024]{1,0:T(8,128)(2,1)} copy(bf16[768,1024]{1,0:T(8,128)(2,1)S(1)} %copy-done) | data formatting | bytes 3145728
Async XLA Ops:
  59.6 4.5 %copy-start = (bf16[768,1024]{1,0:T(8,128)(2,1)S(1)}, bf16[768,1024]{1,0:T(8,128)(2,1)}, u32[]{:S(2)}) copy-start(bf16[768,1024]{1,0:T(8,128)(2,1)} %get-tuple-element.19) | copy-start | bytes 4718596
